TPU v7x, 32 devices: a whole 2x2x4 slice. The times are simulated.
32 devices in a mesh: groups: 2 (over y), expert: 4 (over z), replica: 4 (over x, core).
Axes of the slice: x: 2, y: 2, z: 4, core: 2. Of those that a mesh axis runs over, the one named last changes fastest.
Arguments:
- features: bfloat16 [65536, 256], P(('groups', 'expert', 'replica')), parts along dimension 0, may hold values from -6 to 6
- cotangents: bfloat16 [65536, 256], P(('groups', 'expert', 'replica')), parts along dimension 0, may hold values from -6 to 6
- routes: int32 [65536, 1], P(('groups', 'expert', 'replica')), parts along dimension 0, may hold values from 0 to 3; in each aligned block of 2048 rows (0 to 2047, 2048 to 4095, ...) at most 1024 rows name the same one
- live_counts: int32 [32], P(('groups', 'expert', 'replica')), parts along dimension 0, may hold values from 128 to 2048, as said below
- weights: float32 [8, 4, 256, 256], P(('groups', 'expert')), parts along dimension 0, may hold values from -0.5 to 0.5
- biases: float32 [8, 4, 256], P(('groups', 'expert')), parts along dimension 0, may hold values from -1.8 to 1.8
- first_moment: float32 [8, 4, 256, 256], P(('groups', 'expert'), None, 'replica'), parts along dimension 0, may hold values from -3 to 3
- second_moment: float32 [8, 4, 256, 256], P(('groups', 'expert'), None, 'replica'), parts along dimension 0, may hold values from 0.05 to 1
- bias_first: float32 [8, 4, 256], P(('groups', 'expert'), None, 'replica'), parts along dimension 0, may hold values from -3 to 3
- bias_second: float32 [8, 4, 256], P(('groups', 'expert'), None, 'replica'), parts along dimension 0, may hold values from 0.05 to 1
Outputs:
- input_grads: bfloat16 [65536, 256], P(('groups', 'expert', 'replica')), parts along dimension 0
- new_weights: float32 [8, 4, 256, 256], P(('groups', 'expert'), None, 'replica'), parts along dimension 0
- new_first: float32 [8, 4, 256, 256], P(('groups', 'expert'), None, 'replica'), parts along dimension 0
- new_second: float32 [8, 4, 256, 256], P(('groups', 'expert'), None, 'replica'), parts along dimension 0
- new_biases: float32 [8, 4, 256], P(('groups', 'expert'), None, 'replica'), parts along dimension 0
- new_bias_first: float32 [8, 4, 256], P(('groups', 'expert'), None, 'replica'), parts along dimension 0
- new_bias_second: float32 [8, 4, 256], P(('groups', 'expert'), None, 'replica'), parts along dimension 0
There are 2 independent parts, one for each index of `groups`. A program takes and returns all parts, laid end to end along the dimension named above; each array names one. Nothing has to cross between parts.
Inputs may be any that keep to these rules, and one draw needn't show every extreme that they name: `routes`: among the 2048 rows of one device no expert is named more than 1024 times. `live_counts`: A multiple of 128; some device has all 2048 rows live.
All inputs are finite; a program needn't handle non-finite values.
Results may differ from a plain program's by a relative error of at most 0.0097.
Values may be sent and summed in bfloat16 or wider, within the bound.
A program may use at most 128 MiB of HBM per device.

v0:
```python
import math

import jax
import jax.numpy as jnp
from jax import lax
from jax.sharding import PartitionSpec as P

LAYERS = 4
ROWS_DEV = 2048


beta_first = 0.9
beta_second = 0.999
learn_rate = 0.05
adam_epsilon = 1e-08
first_fix = 1.0 - 0.9**10
second_fix = 1.0 - 0.999**10


def forward_layers(weights_low, bias_rows, inputs_rows):
    activations = [inputs_rows]
    preacts = []
    for layer in range(LAYERS - 1):
        preact = (
            jnp.dot(activations[-1], weights_low[layer], preferred_element_type=jnp.float32)
            + bias_rows[layer]
        )
        preacts.append(preact)
        activations.append(jax.nn.softplus(preact).astype(jnp.bfloat16))
    return (activations, preacts)


def adjoint_chain(weights_low, preacts, adjoint):
    adjoints = [None] * LAYERS
    input_grad = None
    for layer in reversed(range(LAYERS)):
        adjoints[layer] = adjoint
        pulled = lax.dot_general(
            adjoint,
            weights_low[layer],
            (((1,), (1,)), ((), ())),
            preferred_element_type=jnp.float32,
        )
        if layer > 0:
            adjoint = (pulled * jax.nn.sigmoid(preacts[layer - 1])).astype(jnp.bfloat16)
        else:
            input_grad = pulled.astype(jnp.bfloat16)
    return (adjoints, input_grad)


def gradient_terms(activations, adjoints):
    weight_grads = []
    bias_grads = []
    for layer in range(LAYERS):
        weight_grads.append(
            lax.dot_general(
                activations[layer],
                adjoints[layer],
                (((0,), (0,)), ((), ())),
                preferred_element_type=jnp.float32,
            )
        )
        bias_grads.append(jnp.sum(adjoints[layer].astype(jnp.float32), 0))
    return (jnp.stack(weight_grads)[None], jnp.stack(bias_grads)[None])


def adam_update(master, moment_one, moment_two, gradient):
    scaled = gradient / math.sqrt(ROWS_DEV)
    moment_one = beta_first * moment_one + (1.0 - beta_first) * scaled
    moment_two = beta_second * moment_two + (1.0 - beta_second) * scaled * scaled
    updated = master - learn_rate * (moment_one / first_fix) / (
        jnp.sqrt(moment_two / second_fix) + adam_epsilon
    )
    return (updated, moment_one, moment_two)


def shards(
    features,
    cotangents,
    routes,
    live_counts,
    weights,
    biases,
    first_moment,
    second_moment,
    bias_first,
    bias_second,
):
    expert_count = lax.axis_size("expert")
    replicas = lax.axis_size("replica")
    rows_here = features.shape[0]
    feature_width = features.shape[1]
    capacity = 2 * rows_here // expert_count
    route_ids = routes[:, 0]
    positions = lax.iota(jnp.int32, rows_here)
    is_live = positions < live_counts[0]
    masked = jnp.where(is_live[:, None], cotangents, jnp.zeros_like(cotangents))
    onehot = (route_ids[:, None] == lax.iota(jnp.int32, expert_count)[None, :]).astype(jnp.int32)
    weights_low = weights[0].astype(jnp.bfloat16)
    dump_slot = expert_count * capacity
    slot_rank = jnp.sum((jnp.cumsum(onehot, 0) - onehot) * onehot, 1)
    slot_index = route_ids * capacity + slot_rank

    def place(row_data):
        buffer = (
            jnp.zeros((expert_count * capacity, feature_width), row_data.dtype)
            .at[slot_index]
            .set(row_data, mode="drop")
        )
        return buffer.reshape(expert_count, capacity, feature_width)

    got_rows, got_adjoint = (
        lax.all_to_all(place(features), "expert", split_axis=0, concat_axis=0, tiled=True),
        lax.all_to_all(place(masked), "expert", split_axis=0, concat_axis=0, tiled=True),
    )
    inputs_rows = got_rows.reshape(-1, feature_width)
    adjoint = got_adjoint.reshape(-1, feature_width)
    activations, preacts = forward_layers(weights_low, biases[0], inputs_rows)
    adjoints, input_grad = adjoint_chain(weights_low, preacts, adjoint)
    weight_grads, bias_grads = gradient_terms(activations, adjoints)
    returned = lax.all_to_all(
        input_grad.reshape(expert_count, capacity, feature_width),
        "expert",
        split_axis=0,
        concat_axis=0,
        tiled=True,
    )
    flat = returned.reshape(-1, feature_width)
    picked = flat[jnp.minimum(slot_index, dump_slot - 1)]
    input_grads = jnp.where((slot_index < dump_slot)[:, None], picked, jnp.zeros_like(picked))
    shard_rows = feature_width // replicas
    shard_start = lax.axis_index("replica") * shard_rows
    weight_share, bias_share = (
        lax.psum_scatter(
            weight_grads.astype(jnp.bfloat16), "replica", scatter_dimension=2, tiled=True
        ).astype(jnp.float32),
        lax.psum_scatter(
            bias_grads.astype(jnp.bfloat16), "replica", scatter_dimension=2, tiled=True
        ).astype(jnp.float32),
    )
    master_weights = lax.dynamic_slice_in_dim(weights, shard_start, shard_rows, 2)
    master_biases = lax.dynamic_slice_in_dim(biases, shard_start, shard_rows, 2)
    new_weights, new_first, new_second = adam_update(
        master_weights, first_moment, second_moment, weight_share
    )
    new_biases, new_bias_first, new_bias_second = adam_update(
        master_biases, bias_first, bias_second, bias_share
    )
    return (
        input_grads,
        new_weights,
        new_first,
        new_second,
        new_biases,
        new_bias_first,
        new_bias_second,
    )


def solution(mesh):
    return jax.shard_map(
        shards,
        mesh=mesh,
        in_specs=(
            P(("groups", "expert", "replica"), None),
            P(("groups", "expert", "replica"), None),
            P(("groups", "expert", "replica"), None),
            P(("groups", "expert", "replica")),
            P(("groups", "expert"), None, None, None),
            P(("groups", "expert"), None, None),
            P(("groups", "expert"), None, "replica", None),
            P(("groups", "expert"), None, "replica", None),
            P(("groups", "expert"), None, "replica"),
            P(("groups", "expert"), None, "replica"),
        ),
        out_specs=(
            P(("groups", "expert", "replica"), None),
            P(("groups", "expert"), None, "replica", None),
            P(("groups", "expert"), None, "replica", None),
            P(("groups", "expert"), None, "replica", None),
            P(("groups", "expert"), None, "replica"),
            P(("groups", "expert"), None, "replica"),
            P(("groups", "expert"), None, "replica"),
        ),
        check_vma=False,
    )
```

profile of v0, /device:TPU:0, one launch (start us, length us, event | category | flops | bytes accessed | tf_op | source)
XLA Modules:
  0.0 211.2 jit_solution(5193680664055849174)
XLA Ops:
  11.0 11.3 %scatter_custom_fusion.1 = bf16[4096,256]{1,0:T(8,128)(2,1)} fusion(s32[2048]{0:T(1024)S(1)} %bitcast.95, bf16[2048,256]{1,0:T(8,128)(2,1)} %param.10, bf16[]{:T(256)} %constant.22.clone.1), kind=kCustom, calls=%fused_computation.30 | custom fusion | bytes 2097664 | tf_op jit(solution)/shard_map/scatter | solution.py:108
  22.3 6.3 %all-to-all-start.1 = ((bf16[4,1024,256]{2,1,0:T(8,128)(2,1)}), bf16[4,1024,256]{2,1,0:T(8,128)(2,1)S(1)}, u32[]{:S(2)}, u32[]{:S(2)}) async-start(bf16[4,1024,256]{2,1,0:T(8,128)(2,1)} %bitcast.87), calls=%async_computation.1 | async-start | bytes 4194304 | tf_op jit(solution)/shard_map/all_to_all | solution.py:113
  29.4 12.4 %scatter_custom_fusion = bf16[4096,256]{1,0:T(8,128)(2,1)} fusion(s32[2048]{0:T(1024)S(1)} %bitcast.96, bf16[2048,256]{1,0:T(8,128)(2,1)} %param.11, bf16[]{:T(256)} %constant.22.clone.1, pred[2048]{0:T(1024)(128)(4,1)S(1)} %iota_compare_fusion.2), kind=kCustom, calls=%fused_computation.28 | custom fusion | flops 524288 | bytes 3148800 | tf_op jit(solution)/shard_map/scatter | solution.py:108
  41.7 35.1 %all-to-all-done.1 = bf16[4,1024,256]{2,1,0:T(8,128)(2,1)S(1)} async-done(((bf16[4,1024,256]{2,1,0:T(8,128)(2,1)}), bf16[4,1024,256]{2,1,0:T(8,128)(2,1)S(1)}, u32[]{:S(2)}, u32[]{:S(2)}) %all-to-all-start.1) | async-done | bytes 2097184 | tf_op jit(solution)/shard_map/all_to_all | solution.py:113
  76.8 4.5 %all-to-all-start = ((bf16[4,1024,256]{2,1,0:T(8,128)(2,1)}), bf16[4,1024,256]{2,1,0:T(8,128)(2,1)}, u32[]{:S(2)}, u32[]{:S(2)}) async-start(bf16[4,1024,256]{2,1,0:T(8,128)(2,1)} %bitcast.86), calls=%async_computation | async-start | bytes 4194304 | tf_op jit(solution)/shard_map/all_to_all | solution.py:114
  82.3 2.5 %convolution_add_fusion.1 = f32[4096,256]{1,0:T(8,128)S(1)} fusion(f32[256]{0:T(256)S(1)} %bitcast.99, bf16[1,4,256,256]{3,2,1,0:T(8,128)(2,1)S(1)} %convert_element_type.71, f32[4096,256]{1,0:T(8,128)S(1)} %convolution_add_fusion.2), kind=kOutput, calls=%fused_computation.9 | convolution fusion | flops 545259520 | bytes 8520704 | tf_op jit(solution)/shard_map/dot_general | solution.py:25
  84.8 2.0 copy-done.8
  86.8 4.5 %convolution_add_fusion = f32[4096,256]{1,0:T(8,128)} fusion(f32[256]{0:T(256)S(1)} %bitcast.98, bf16[1,4,256,256]{3,2,1,0:T(8,128)(2,1)S(1)} %convert_element_type.71, f32[4096,256]{1,0:T(8,128)S(1)} %convolution_add_fusion.1), kind=kOutput, calls=%fused_computation.8 | convolution fusion | flops 545259520 | bytes 8520704 | tf_op jit(solution)/shard_map/dot_general | solution.py:25
  91.3 37.8 %all-to-all-done = bf16[4,1024,256]{2,1,0:T(8,128)(2,1)} async-done(((bf16[4,1024,256]{2,1,0:T(8,128)(2,1)}), bf16[4,1024,256]{2,1,0:T(8,128)(2,1)}, u32[]{:S(2)}, u32[]{:S(2)}) %all-to-all-start) | async-done | bytes 2097184 | tf_op jit(solution)/shard_map/all_to_all | solution.py:114
  129.0 4.3 %fusion.44 = (bf16[256]{0:T(256)(128)(2,1)S(1)}, bf16[4096,256]{1,0:T(8,128)(2,1)S(1)}) fusion(f32[4096,256]{1,0:T(8,128)} %convolution_add_fusion, bf16[4096,256]{1,0:T(8,128)(2,1)} %bitcast.7, bf16[1,4,256,256]{3,2,1,0:T(8,128)(2,1)} %copy-done.4), kind=kOutput, calls=%fused_computation.75 | convolution fusion | flops 543162112 | bytes 8520192 | tf_op jit(solution)/shard_map/dot_general | solution.py:38
  133.4 1.3 fusion.45
  134.7 2.4 %copy-done.1 = f32[4096,256]{1,0:T(8,128)S(1)} copy-done((f32[4096,256]{1,0:T(8,128)S(1)}, f32[4096,256]{1,0:T(8,128)}, u32[]{:S(2)}) %copy-start.1) | copy-done | bytes 4194328
  139.1 2.1 convolution_convert_fusion
  141.2 2.1 %reduce.4 = bf16[256]{0:T(256)(128)(2,1)S(1)} reduce(bf16[4,1024,256]{2,1,0:T(8,128)(2,1)} %all-to-all-done, bf16[]{:T(256)} %constant.22.clone.1), dimensions={0,1}, to_apply=%region_9.10.clone | reduce | flops 1048320 | bytes 2097666 | tf_op jit(solution)/shard_map/reduce_sum | solution.py:63
  144.3 3.6 %all-to-all-start.2 = ((bf16[4,1024,256]{2,1,0:T(8,128)(2,1)}), bf16[4,1024,256]{2,1,0:T(8,128)(2,1)S(1)}, u32[]{:S(2)}, u32[]{:S(2)}) async-start(bf16[4,1024,256]{2,1,0:T(8,128)(2,1)} %bitcast.83), calls=%async_computation.2 | async-start | bytes 4194304 | tf_op jit(solution)/shard_map/all_to_all | solution.py:121
  148.2 5.6 %fusion.14 = bf16[1,1,256,256]{3,2,1,0:T(8,128)(2,1)S(1)} fusion(bf16[4096,256]{1,0:T(8,128)(2,1)} %bitcast.7, f32[4096,256]{1,0:T(8,128)} %convolution_add_fusion), kind=kOutput, calls=%fused_computation.27 | convolution fusion | flops 544276480 | bytes 6422528 | tf_op jit(solution)/shard_map/dot_general | solution.py:56
  153.9 2.6 %fusion.13 = bf16[1,1,256,256]{3,2,1,0:T(8,128)(2,1)S(1)} fusion(bf16[4096,256]{1,0:T(8,128)(2,1)S(1)} %copy-done.12, f32[4096,256]{1,0:T(8,128)S(1)} %copy-done.10), kind=kOutput, calls=%fused_computation.26 | convolution fusion | flops 544276480 | bytes 6422528 | tf_op jit(solution)/shard_map/dot_general | solution.py:56
  156.8 2.6 %fusion.12 = bf16[1,1,256,256]{3,2,1,0:T(8,128)(2,1)S(1)} fusion(bf16[4096,256]{1,0:T(8,128)(2,1)S(1)} %copy-done.14, f32[4096,256]{1,0:T(8,128)S(1)} %copy-done.2), kind=kOutput, calls=%fused_computation.25 | convolution fusion | flops 544276480 | bytes 6422528 | tf_op jit(solution)/shard_map/dot_general | solution.py:56
  160.2 2.8 %reduce-scatter.7.cloned.1.call-done = bf16[64,4]{1,0:T(8,128)(2,1)} async-done(((bf16[256,4]{1,0:T(8,128)(2,1)}), bf16[64,4]{1,0:T(8,128)(2,1)}) %reduce-scatter.7.cloned.1.call-update) | async-done | bytes 528
  163.8 1.4 divide_subtract_fusion.1
  165.2 22.7 %reduce-scatter.5.cloned.1.call-done = bf16[1,4,64,256]{3,2,1,0:T(8,128)(2,1)} async-done(((bf16[1,4,256,256]{3,2,1,0:T(8,128)(2,1)}), bf16[1,4,64,256]{3,2,1,0:T(8,128)(2,1)}) %reduce-scatter.5.cloned.1.call-update) | async-done | bytes 131088 | tf_op jit(solution)/shard_map/reduce_scatter | solution.py:134
  187.9 2.0 divide_subtract_fusion
  189.9 5.7 %all-to-all-done.2 = bf16[4,1024,256]{2,1,0:T(8,128)(2,1)S(1)} async-done(((bf16[4,1024,256]{2,1,0:T(8,128)(2,1)}), bf16[4,1024,256]{2,1,0:T(8,128)(2,1)S(1)}, u32[]{:S(2)}, u32[]{:S(2)}) %all-to-all-start.2) | async-done | bytes 2097184 | tf_op jit(solution)/shard_map/all_to_all | solution.py:121
  195.6 7.5 %gather_fusion = bf16[2048,256]{1,0:T(8,128)(2,1)S(1)} fusion(bf16[4096,256]{1,0:T(8,128)(2,1)S(1)} %bitcast.82, s32[2048]{0:T(1024)S(1)} %broadcast_clamp_fusion), kind=kCustom, calls=%fused_computation | custom fusion | bytes 2105344 | tf_op jit(solution)/shard_map/gather | solution.py:129
  (58 shorter events, 11.3 us)
Async XLA Ops:
  22.3 54.5 %all-to-all-start.1 = ((bf16[4,1024,256]{2,1,0:T(8,128)(2,1)}), bf16[4,1024,256]{2,1,0:T(8,128)(2,1)S(1)}, u32[]{:S(2)}, u32[]{:S(2)}) async-start(bf16[4,1024,256]{2,1,0:T(8,128)(2,1)} %bitcast.87), calls=%async_computation.1 | async-start | bytes 4194304 | tf_op jit(solution)/shard_map/all_to_all | solution.py:113
  28.6 52.9 %copy-start.3 = (f32[1,4,256,256]{3,2,1,0:T(8,128)S(1)}, f32[1,4,256,256]{3,2,1,0:T(8,128)}, u32[]{:S(2)}) copy-start(f32[1,4,256,256]{3,2,1,0:T(8,128)} %param.14) | copy-start | bytes 3145732
  29.4 52.2 %copy-start.7 = (f32[1,4,256]{2,1,0:T(4,128)S(1)}, f32[1,4,256]{2,1,0:T(4,128)}, u32[]{:S(2)}) copy-start(f32[1,4,256]{2,1,0:T(4,128)} %param.15) | copy-start | bytes 12292
  76.8 52.2 %all-to-all-start = ((bf16[4,1024,256]{2,1,0:T(8,128)(2,1)}), bf16[4,1024,256]{2,1,0:T(8,128)(2,1)}, u32[]{:S(2)}, u32[]{:S(2)}) async-start(bf16[4,1024,256]{2,1,0:T(8,128)(2,1)} %bitcast.86), calls=%async_computation | async-start | bytes 4194304 | tf_op jit(solution)/shard_map/all_to_all | solution.py:114
  81.3 81.7 %reduce-scatter.7.cloned.1.call-start = ((), (), s32[]{:S(2)}) async-start(), calls=%async_computation.6 | async-start | bytes 81920
  81.6 3.2 %copy-start.4 = (bf16[1,4,256,256]{3,2,1,0:T(8,128)(2,1)}, bf16[1,4,256,256]{3,2,1,0:T(8,128)(2,1)S(1)}, u32[]{:S(2)}) copy-start(bf16[1,4,256,256]{3,2,1,0:T(8,128)(2,1)S(1)} %convert_element_type.71) | copy-start | bytes 1572868
  82.3 2.5 %copy-start = (f32[4096,256]{1,0:T(8,128)}, f32[4096,256]{1,0:T(8,128)S(1)}, u32[]{:S(2)}) copy-start(f32[4096,256]{1,0:T(8,128)S(1)} %convolution_add_fusion.2) | copy-start | bytes 12582916
  84.8 2.0 copy-start.8
  129.0 4.3 %copy-start.5 = (bf16[1,4,256,256]{3,2,1,0:T(8,128)(2,1)S(1)}, bf16[1,4,256,256]{3,2,1,0:T(8,128)(2,1)}, u32[]{:S(2)}) copy-start(bf16[1,4,256,256]{3,2,1,0:T(8,128)(2,1)} %copy-done.4) | copy-start | bytes 1572868
  129.0 4.3 %copy-start.9 = (f32[4096,256]{1,0:T(8,128)S(1)}, f32[4096,256]{1,0:T(8,128)}, u32[]{:S(2)}) copy-start(f32[4096,256]{1,0:T(8,128)} %copy-done.8) | copy-start | bytes 12582916
  133.3 1.3 copy-start.11
  133.4 3.7 %copy-start.1 = (f32[4096,256]{1,0:T(8,128)S(1)}, f32[4096,256]{1,0:T(8,128)}, u32[]{:S(2)}) copy-start(f32[4096,256]{1,0:T(8,128)} %copy-done) | copy-start | bytes 12582916
  134.7 3.7 %copy-start.13 = (bf16[4096,256]{1,0:T(8,128)(2,1)}, bf16[4096,256]{1,0:T(8,128)(2,1)S(1)}, u32[]{:S(2)}) copy-start(bf16[4096,256]{1,0:T(8,128)(2,1)S(1)} %get-tuple-element.23) | copy-start | bytes 6291460
  144.3 51.3 %all-to-all-start.2 = ((bf16[4,1024,256]{2,1,0:T(8,128)(2,1)}), bf16[4,1024,256]{2,1,0:T(8,128)(2,1)S(1)}, u32[]{:S(2)}, u32[]{:S(2)}) async-start(bf16[4,1024,256]{2,1,0:T(8,128)(2,1)} %bitcast.83), calls=%async_computation.2 | async-start | bytes 4194304 | tf_op jit(solution)/shard_map/all_to_all | solution.py:121
  147.9 40.0 %reduce-scatter.5.cloned.1.call-start = ((), (), s32[]{:S(2)}) async-start(), calls=%async_computation.5 | async-start | bytes 655360 | tf_op jit(solution)/shard_map/reduce_scatter | solution.py:134
  148.2 5.7 %copy-start.10 = (f32[4096,256]{1,0:T(8,128)S(1)}, f32[4096,256]{1,0:T(8,128)}, u32[]{:S(2)}) copy-start(f32[4096,256]{1,0:T(8,128)} %copy-done.8) | copy-start | bytes 12582916
  148.2 5.7 %copy-start.12 = (bf16[4096,256]{1,0:T(8,128)(2,1)S(1)}, bf16[4096,256]{1,0:T(8,128)(2,1)}, u32[]{:S(2)}) copy-start(bf16[4096,256]{1,0:T(8,128)(2,1)} %copy-done.11) | copy-start | bytes 6291460
  153.9 2.6 %copy-start.2 = (f32[4096,256]{1,0:T(8,128)S(1)}, f32[4096,256]{1,0:T(8,128)}, u32[]{:S(2)}) copy-start(f32[4096,256]{1,0:T(8,128)} %copy-done) | copy-start | bytes 12582916
  153.9 2.9 %copy-start.14 = (bf16[4096,256]{1,0:T(8,128)(2,1)S(1)}, bf16[4096,256]{1,0:T(8,128)(2,1)}, u32[]{:S(2)}) copy-start(bf16[4096,256]{1,0:T(8,128)(2,1)} %copy-done.13) | copy-start | bytes 6291460
  156.7 31.1 %copy-start.6 = (f32[1,4,64,256]{3,2,1,0:T(8,128)S(1)}, f32[1,4,64,256]{3,2,1,0:T(8,128)}, u32[]{:S(2)}) copy-start(f32[1,4,64,256]{3,2,1,0:T(8,128)} %param.16) | copy-start | bytes 786436
Sparse Core Ops, SparseCore 0:
  144.4 18.5 reduce-scatter.6
  166.2 21.6 reduce-scatter.4
where the time goes:
time: 212 us; the launch traced here: 211 us
  waiting for transfers between devices  104 us (49%)
  matrix products  28.2 us (13%)
  local copies, waits for them, and re-layouts  25.3 us (12%)
  other arithmetic  23.7 us (11%)
  between operations  15.1 us (7%)
  starting transfers between devices  14.9 us (7%)
    all_to_all x1, waiting for transfers between devices, shards(): lax.all_to_all(place(masked), 'expert', split_axis=0, concat_axis=0, tile...  37.8 us
    all_to_all x1, waiting for transfers between devices, shards(): lax.all_to_all(place(features), 'expert', split_axis=0, concat_axis=0, ti...  35.1 us
    reduce_scatter x1, waiting for transfers between devices, shards(): lax.psum_scatter(weight_grads.astype(jnp.bfloat16), 'replica', scatter_di...  22.7 us
    scatter x1, other arithmetic, place(): buffer = jnp.zeros((expert_count * capacity, feature_width), row_data.dty...  12.4 us
    dot_general x4, matrix products, gradient_terms(): lax.dot_general(activations[layer], adjoints[layer], (((0,), (0,)), ((),...  11.6 us
    scatter x1, local copies, waits for them, and re-layouts, place(): buffer = jnp.zeros((expert_count * capacity, feature_width), row_data.dty...  11.3 us
    dot_general x4, matrix products, adjoint_chain(): lax.dot_general(adjoint, weights_low[layer], (((1,), (1,)), ((), ())), pr...  8.97 us
    dot_general x3, matrix products, forward_layers(): jnp.dot(activations[-1], weights_low[layer], preferred_element_type=jnp.f...  7.64 us
  transfers between devices with their start and end apart: 5, of which 5 were waited for; matrix products, arithmetic and copies ran while one was open for 17% of the time, Pallas kernels for 0%

commit v1 on v0

--- a/solution.py
+++ b/solution.py
@@ -1,8 +1,11 @@
+import functools
 import math
 
 import jax
 import jax.numpy as jnp
 from jax import lax
+from jax.experimental import pallas as pl
+from jax.experimental.pallas import tpu as pltpu
 from jax.sharding import PartitionSpec as P
 
 LAYERS = 4
@@ -74,7 +77,7 @@
     return (updated, moment_one, moment_two)
 
 
-def shards(
+def routed_shards(
     features,
     cotangents,
     routes,
@@ -155,6 +158,460 @@
         new_bias_first,
         new_bias_second,
     )
+
+
+TILE = 512
+SLICE = 64
+TAIL = 16
+
+
+def softplus_and_sigmoid(x):
+    small = jnp.exp(-jnp.abs(x))
+    total = 1.0 + small
+    inverse = pl.reciprocal(total)
+    log_part = jnp.where(small < 1e-3, small - 0.5 * small * small, jnp.log(total))
+    return jnp.maximum(x, 0.0) + log_part, jnp.where(x >= 0.0, inverse, small * inverse)
+
+
+def fused_kernel(
+    experts,
+    live_ref,
+    features_ref,
+    cotangents_ref,
+    routes_ref,
+    weights_ref,
+    biases_ref,
+    first_ref,
+    second_ref,
+    bias_first_ref,
+    bias_second_ref,
+    input_grads_ref,
+    new_weights_ref,
+    new_first_ref,
+    new_second_ref,
+    new_biases_ref,
+    new_bias_first_ref,
+    new_bias_second_ref,
+    low,
+    bias_all,
+    onehot,
+    mask,
+    acts,
+    sigs,
+    adj,
+    grad,
+    bias_grad,
+    core_send,
+    core_recv,
+    core_keep,
+    chip_send,
+    chip_recv,
+    chip_keep,
+    line_send,
+    line_recv,
+    z_sems,
+    x_sems,
+    c_sems,
+    b_sems,
+    core_sems,
+    chip_sems,
+    line_sems,
+):
+    rows, width = features_ref.shape
+    wide = experts * width
+    tiles = rows // TILE
+    expert = lax.axis_index("expert")
+    replica = lax.axis_index("replica")
+    chip, core = replica // 2, replica % 2
+    other_core = {"replica": chip * 2 + 1 - core}
+    other_chip = {"replica": (1 - chip) * 2 + core}
+    others = range(1, experts)
+
+    def along(d):
+        return {"expert": lax.rem(expert + d, experts)}
+
+    def before(d):
+        return lax.rem(expert + d, experts)
+
+    barrier = pltpu.get_barrier_semaphore()
+    for peer in [other_core, other_chip] + [along(d) for d in others]:
+        pl.semaphore_signal(barrier, inc=1, device_id=peer, device_id_type=pl.DeviceIdType.MESH)
+    for layer in range(LAYERS):
+        low[layer, expert] = weights_ref[layer].astype(jnp.bfloat16)
+    bias_all[expert] = jnp.concatenate([biases_ref[...], jnp.zeros_like(biases_ref)], 0)
+    pl.semaphore_wait(barrier, experts + 1)
+
+    started = []
+
+    def send(src, dst, sems, index, peer):
+        copy = pltpu.make_async_remote_copy(
+            src_ref=src,
+            dst_ref=dst,
+            send_sem=sems.at[(0,) + index],
+            recv_sem=sems.at[(1,) + index],
+            device_id=peer,
+            device_id_type=pl.DeviceIdType.MESH,
+        )
+        copy.start()
+        started.append(copy)
+        return copy
+
+    own_start = pl.multiple_of(core * 2 * SLICE + chip * SLICE, SLICE)
+    half_start = pl.multiple_of(core * 2 * SLICE, 2 * SLICE)
+    bias_copies = []
+    line_copies = []
+    for layer in range(LAYERS):
+        quarter = low.at[layer, expert, pl.ds(own_start, SLICE)]
+        line_copies.append([send(quarter, quarter, z_sems, (layer, d - 1), along(d)) for d in others])
+        if layer == 0:
+            whole = bias_all.at[expert]
+            bias_copies = [send(whole, whole, b_sems, (d - 1,), along(d)) for d in others]
+
+    chip_copies = {}
+    core_copies = {}
+
+    def pass_to_chip(layer):
+        chip_copies[layer] = []
+        for copy in line_copies[layer]:
+            copy.wait_recv()
+        for d in others:
+            part = low.at[layer, before(d), pl.ds(own_start, SLICE)]
+            chip_copies[layer].append(send(part, part, x_sems, (layer, d - 1), other_chip))
+
+    def pass_to_core(layer):
+        core_copies[layer] = []
+        for copy in chip_copies[layer]:
+            copy.wait_recv()
+        for d in others:
+            part = low.at[layer, before(d), pl.ds(half_start, 2 * SLICE)]
+            core_copies[layer].append(send(part, part, c_sems, (layer, d - 1), other_core))
+
+    def arrived(layer):
+        for copy in core_copies[layer]:
+            copy.wait_recv()
+
+    def each_tile(body):
+        def step(i, carry):
+            body(pl.ds(pl.multiple_of(i * TILE, TILE), TILE))
+            return carry
+
+        lax.fori_loop(0, tiles, step, 0)
+
+    row_of = lax.broadcasted_iota(jnp.int32, (16, rows), 0)
+    position = lax.broadcasted_iota(jnp.int32, (16, rows), 1)
+    named = (routes_ref[...] == row_of % experts) & (row_of < 3 * experts)
+    named = named & (position < live_ref[0])
+    onehot[...] = jnp.where(named, 1.0, 0.0).astype(jnp.bfloat16)
+    spread_row = lax.broadcasted_iota(jnp.int32, (16, wide), 0)
+    spread_column = lax.broadcasted_iota(jnp.int32, (16, wide), 1)
+    spread = jnp.where(spread_row == spread_column // width, 1.0, 0.0).astype(jnp.bfloat16)
+    contract_rows = (((0,), (0,)), ((), ()))
+
+    for copy in bias_copies:
+        copy.wait_recv()
+    bias_parts = []
+    for layer in range(LAYERS - 1):
+        whole = jnp.concatenate([bias_all[e, layer : layer + 1] for e in range(experts)], 0)
+        high = whole.astype(jnp.bfloat16).astype(jnp.float32)
+        middle = (whole - high).astype(jnp.bfloat16).astype(jnp.float32)
+        lowest = whole - high - middle
+        bias_parts.append(
+            jnp.concatenate([high, middle, lowest, jnp.zeros_like(high)], 0).astype(jnp.bfloat16)
+        )
+
+    def prepare(at):
+        chosen = onehot[:, at]
+        mask[at, :] = lax.dot_general(
+            chosen, spread, contract_rows, preferred_element_type=jnp.float32
+        ).astype(jnp.bfloat16)
+        for layer in range(LAYERS - 1):
+            sigs[layer, at, :] = lax.dot_general(
+                chosen, bias_parts[layer], contract_rows, preferred_element_type=jnp.float32
+            )
+
+    each_tile(prepare)
+
+    def separated(block, at):
+        return jnp.concatenate([block] * experts, 1) * mask[at, :]
+
+    def forward(layer):
+        def body(at):
+            block = features_ref[at, :] if layer == 0 else acts[layer - 1, at, :]
+            preact = (
+                jnp.dot(
+                    separated(block, at),
+                    low[layer].reshape(wide, width),
+                    preferred_element_type=jnp.float32,
+                )
+                + sigs[layer, at, :]
+            )
+            soft, sig = softplus_and_sigmoid(preact)
+            acts[layer, at, :] = soft.astype(jnp.bfloat16)
+            sigs[layer, at, :] = sig
+
+        each_tile(body)
+
+    pass_to_chip(0)
+    pass_to_chip(1)
+    pass_to_core(0)
+    arrived(0)
+    forward(0)
+    pass_to_chip(2)
+    pass_to_core(1)
+    pass_to_chip(3)
+    arrived(1)
+    forward(1)
+    pass_to_core(2)
+    pass_to_core(3)
+    arrived(2)
+    forward(2)
+    arrived(3)
+
+    def adjoint_of(layer, at):
+        return cotangents_ref[at, :] if layer == LAYERS - 1 else adj[at, :]
+
+    def gradients(layer):
+        grad[...] = jnp.zeros_like(grad)
+        bias_grad[layer] = jnp.zeros((16, width), jnp.float32)
+
+        def body(at):
+            block = adjoint_of(layer, at)
+            act = features_ref[at, :] if layer == 0 else acts[layer - 1, at, :]
+            grad[...] += lax.dot_general(
+                act, separated(block, at), contract_rows, preferred_element_type=jnp.float32
+            )
+            bias_grad[layer] += jnp.dot(onehot[:, at], block, preferred_element_type=jnp.float32)
+
+        each_tile(body)
+
+    def pull(layer):
+        def body(at):
+            parts = separated(adjoint_of(layer, at), at)
+            pulled = sum(
+                lax.dot_general(
+                    parts[:, e * width : (e + 1) * width],
+                    low[layer, e],
+                    (((1,), (1,)), ((), ())),
+                    preferred_element_type=jnp.float32,
+                )
+                for e in range(experts)
+            )
+            if layer > 0:
+                adj[at, :] = (pulled * sigs[layer - 1, at, :]).astype(jnp.bfloat16)
+            else:
+                input_grads_ref[at, :] = pulled.astype(jnp.bfloat16)
+
+        each_tile(body)
+
+    def height(layer):
+        return SLICE + (TAIL if layer == 0 else 0)
+
+    sums = {}
+
+    def share_core(layer):
+        for e in range(experts):
+            columns = slice(e * width, (e + 1) * width)
+            if layer == 0:
+                tail = jnp.concatenate(
+                    [bias_grad[k, e : e + 1] for k in range(LAYERS)]
+                    + [jnp.zeros((TAIL - LAYERS, width), jnp.float32)],
+                    0,
+                )
+            for c in range(2):
+                mine = pl.ds(pl.multiple_of((c * 2 + core) * SLICE, SLICE), SLICE)
+                theirs = pl.ds(pl.multiple_of((c * 2 + 1 - core) * SLICE, SLICE), SLICE)
+                core_keep[layer, c, e, :SLICE] = grad[mine, columns]
+                core_send[layer, c, e, :SLICE] = grad[theirs, columns].astype(jnp.bfloat16)
+                if layer == 0:
+                    core_keep[layer, c, e, SLICE:] = tail
+                    core_send[layer, c, e, SLICE:] = tail.astype(jnp.bfloat16)
+        part = pl.ds(0, height(layer))
+        sums["core", layer] = send(
+            core_send.at[layer, :, :, part],
+            core_recv.at[layer, :, :, part],
+            core_sems,
+            (layer,),
+            other_core,
+        )
+
+    def share_chip(layer):
+        sums["core", layer].wait_recv()
+        n = height(layer)
+        for e in range(experts):
+            chip_send[layer, e, :n] = (
+                core_keep[layer, 1 - chip, e, :n]
+                + core_recv[layer, 1 - chip, e, :n].astype(jnp.float32)
+            ).astype(jnp.bfloat16)
+        part = pl.ds(0, n)
+        sums["chip", layer] = send(
+            chip_send.at[layer, :, part], chip_recv.at[layer, :, part], chip_sems, (layer,), other_chip
+        )
+        for e in range(experts):
+            chip_keep[layer, e, :n] = core_keep[layer, chip, e, :n] + core_recv[
+                layer, chip, e, :n
+            ].astype(jnp.float32)
+
+    def share_line(layer):
+        sums["chip", layer].wait_recv()
+        n = height(layer)
+        for e in range(experts):
+            total = chip_keep[layer, e, :n] + chip_recv[layer, e, :n].astype(jnp.float32)
+            chip_keep[layer, e, :n] = total
+            line_send[layer, e, :n] = total.astype(jnp.bfloat16)
+        part = pl.ds(0, n)
+        sums["line", layer] = [
+            send(
+                line_send.at[layer, before(d), part],
+                line_recv.at[layer, d - 1, part],
+                line_sems,
+                (layer, d - 1),
+                along(d),
+            )
+            for d in others
+        ]
+
+    def finish(layer):
+        for copy in sums["line", layer]:
+            copy.wait_recv()
+        n = height(layer)
+        total = chip_keep[layer, expert, :n]
+        for d in others:
+            total = total + line_recv[layer, d - 1, :n].astype(jnp.float32)
+        master = weights_ref[layer, pl.ds(pl.multiple_of(replica * SLICE, SLICE), SLICE), :]
+        updated, one, two = adam_update(master, first_ref[layer], second_ref[layer], total[:SLICE])
+        new_weights_ref[layer] = updated
+        new_first_ref[layer] = one
+        new_second_ref[layer] = two
+        if layer == 0:
+
+            def own_columns(block):
+                picked = block[:, :SLICE]
+                for k in range(1, width // SLICE):
+                    picked = jnp.where(replica == k, block[:, k * SLICE : (k + 1) * SLICE], picked)
+                return picked
+
+            updated, one, two = adam_update(
+                own_columns(biases_ref[...]),
+                bias_first_ref[...],
+                bias_second_ref[...],
+                own_columns(total[SLICE : SLICE + LAYERS]),
+            )
+            new_biases_ref[...] = updated
+            new_bias_first_ref[...] = one
+            new_bias_second_ref[...] = two
+
+    gradients(3)
+    share_core(3)
+    pull(3)
+    share_chip(3)
+    gradients(2)
+    share_core(2)
+    share_line(3)
+    pull(2)
+    share_chip(2)
+    gradients(1)
+    share_core(1)
+    share_line(2)
+    pull(1)
+    share_chip(1)
+    gradients(0)
+    share_core(0)
+    share_line(1)
+    pull(0)
+    share_chip(0)
+    finish(3)
+    finish(2)
+    share_line(0)
+    finish(1)
+    finish(0)
+    for copy in started:
+        copy.wait_send()
+
+
+def fused_shards(
+    features,
+    cotangents,
+    routes,
+    live_counts,
+    weights,
+    biases,
+    first_moment,
+    second_moment,
+    bias_first,
+    bias_second,
+):
+    experts = lax.axis_size("expert")
+    rows, width = features.shape
+    wide = experts * width
+    tall = SLICE + TAIL
+    f32, bf16 = jnp.float32, jnp.bfloat16
+    vmem = pl.BlockSpec(memory_space=pltpu.VMEM)
+    moment = jax.ShapeDtypeStruct(first_moment.shape[1:], f32)
+    bias_moment = jax.ShapeDtypeStruct(bias_first.shape[1:], f32)
+    outs = pl.pallas_call(
+        functools.partial(fused_kernel, experts),
+        out_shape=(
+            jax.ShapeDtypeStruct((rows, width), bf16),
+            moment,
+            moment,
+            moment,
+            bias_moment,
+            bias_moment,
+            bias_moment,
+        ),
+        in_specs=[pl.BlockSpec(memory_space=pltpu.SMEM)] + [vmem] * 9,
+        out_specs=(vmem,) * 7,
+        scratch_shapes=[
+            pltpu.VMEM((LAYERS, experts, width, width), bf16),
+            pltpu.VMEM((experts, 2 * LAYERS, width), f32),
+            pltpu.VMEM((16, rows), bf16),
+            pltpu.VMEM((rows, wide), bf16),
+            pltpu.VMEM((LAYERS - 1, rows, width), bf16),
+            pltpu.VMEM((LAYERS - 1, rows, width), f32),
+            pltpu.VMEM((rows, width), bf16),
+            pltpu.VMEM((width, wide), f32),
+            pltpu.VMEM((LAYERS, 16, width), f32),
+            pltpu.VMEM((LAYERS, 2, experts, tall, width), bf16),
+            pltpu.VMEM((LAYERS, 2, experts, tall, width), bf16),
+            pltpu.VMEM((LAYERS, 2, experts, tall, width), f32),
+            pltpu.VMEM((LAYERS, experts, tall, width), bf16),
+            pltpu.VMEM((LAYERS, experts, tall, width), bf16),
+            pltpu.VMEM((LAYERS, experts, tall, width), f32),
+            pltpu.VMEM((LAYERS, experts, tall, width), bf16),
+            pltpu.VMEM((LAYERS, experts - 1, tall, width), bf16),
+            pltpu.SemaphoreType.DMA((2, LAYERS, experts - 1)),
+            pltpu.SemaphoreType.DMA((2, LAYERS, experts - 1)),
+            pltpu.SemaphoreType.DMA((2, LAYERS, experts - 1)),
+            pltpu.SemaphoreType.DMA((2, experts - 1)),
+            pltpu.SemaphoreType.DMA((2, LAYERS)),
+            pltpu.SemaphoreType.DMA((2, LAYERS)),
+            pltpu.SemaphoreType.DMA((2, LAYERS, experts - 1)),
+        ],
+        compiler_params=pltpu.CompilerParams(
+            collective_id=0, has_side_effects=True, vmem_limit_bytes=56 * 1024 * 1024
+        ),
+        cost_estimate=pl.CostEstimate(
+            flops=22 * rows * wide * width, bytes_accessed=6 * 2**20, transcendentals=9 * rows * width
+        ),
+    )(
+        live_counts,
+        features,
+        cotangents,
+        routes.reshape(1, rows),
+        weights[0],
+        biases[0],
+        first_moment[0],
+        second_moment[0],
+        bias_first[0],
+        bias_second[0],
+    )
+    return (outs[0],) + tuple(out[None] for out in outs[1:])
+
+
+def shards(*arrays):
+    if lax.axis_size("expert") == 4 and lax.axis_size("replica") == 4:
+        return fused_shards(*arrays)
+    return routed_shards(*arrays)
 
 
 def solution(mesh):

time: 212 us -> 75.6 us (0.36)
  waiting for transfers between devices: 104 us -> 0 us
  Pallas kernels: 0 us -> 67 us
  matrix products: 28.2 us -> 0 us
  other arithmetic: 23.7 us -> 0 us
  local copies, waits for them, and re-layouts: 25.3 us -> 7.02 us
  starting transfers between devices: 14.9 us -> 0 us
  between operations: 15.1 us -> 1.31 us
    all_to_all x3 -> x0, waiting for transfers between devices: 78.5 us -> none  [the longest x1 37.8 us: shards(): lax.all_to_all(place(masked), 'expert', split_axis=0, concat_axis=0, tile...]
    pallas_call x0 -> x1, Pallas kernels: none -> 67 us  [fused_shards(): pl.pallas_call(functools.partial(fused_kernel, experts), out_shape=(jax.S...]
    dot_general x11 -> x0, matrix products: 28.2 us -> none  [the longest x4 11.6 us: gradient_terms(): lax.dot_general(activations[layer], adjoints[layer], (((0,), (0,)), ((),...]
    reduce_scatter x1 -> x0, waiting for transfers between devices: 22.7 us -> none  [shards(): lax.psum_scatter(weight_grads.astype(jnp.bfloat16), 'replica', scatter_di...]
    all_to_all x3 -> x0, starting transfers between devices: 14.4 us -> none  [the longest x1 6.32 us: shards(): lax.all_to_all(place(features), 'expert', split_axis=0, concat_axis=0, ti...]
    scatter x1 -> x0, other arithmetic: 12.4 us -> none  [place(): buffer = jnp.zeros((expert_count * capacity, feature_width), row_data.dty...]
    scatter x1 -> x0, local copies, waits for them, and re-layouts: 11.3 us -> none  [place(): buffer = jnp.zeros((expert_count * capacity, feature_width), row_data.dty...]
    gather x1 -> x0, local copies, waits for them, and re-layouts: 7.49 us -> none  [shards(): picked = flat[jnp.minimum(slot_index, dump_slot - 1)]]
  transfers between devices with their start and end apart: 5 -> 0, of which waited for: 5 -> 0; matrix products, arithmetic and copies ran while one was open for 17% -> 0% of each run, Pallas kernels for 0% -> 0%
where the time goes in v1:
time: 75.6 us; the launch traced here: 75.3 us
  Pallas kernels  67 us (89%)
  local copies, waits for them, and re-layouts  7.02 us (9%)
  between operations  1.31 us (2%)
    pallas_call x1, Pallas kernels, fused_shards(): pl.pallas_call(functools.partial(fused_kernel, experts), out_shape=(jax.S...  67 us
    unnamed x19, local copies, waits for them, and re-layouts  7.02 us

profile of v1, /device:TPU:0, one launch (start us, length us, event | category | flops | bytes accessed | tf_op | source)
XLA Modules:
  0.0 75.3 jit_solution(434746598905495500)
XLA Ops:
  1.3 67.0 %shard_map.153 = (bf16[2048,256]{1,0:T(8,128)(2,1)}, f32[4,64,256]{2,1,0:T(8,128)}, f32[4,64,256]{2,1,0:T(8,128)}, f32[4,64,256]{2,1,0:T(8,128)}, f32[4,64]{1,0:...) custom-call(s32[1]{0:T(128)S(6)} %copy.24.live_ref, bf16[2048,256]{1,0:T(8,128)(2,1)} %features_ref.1, ...), custom_call_target="tpu_custom_call" | custom-call | flops 11811160064 | bytes 6291456 | tf_op jit(solution)/shard_map/pallas_call | solution.py:551
  68.3 0.0 copy-start.2
  68.3 2.3 %copy.25 = bf16[2048,256]{1,0:T(8,128)(2,1)} copy(bf16[2048,256]{1,0:T(8,128)(2,1)} %get-tuple-element.28) | data formatting | bytes 2097152
  70.6 0.0 copy-done.2
  70.6 0.0 copy-start.1
  70.6 0.7 copy.26
  71.3 0.3 copy-done.1
  71.6 0.0 copy-start
  71.6 0.7 copy.27
  72.3 0.3 copy-done
  72.7 0.0 copy-start.5
  72.7 0.7 copy.28
  73.4 0.0 copy-done.5
  73.4 0.0 copy-start.4
  73.4 0.6 copy.29
  73.9 0.1 copy-done.4
  74.0 0.0 copy-start.3
  74.0 0.6 copy.30
  74.6 0.1 copy-done.3
  74.7 0.6 copy.31
Async XLA Ops:
  68.3 2.3 %copy-start.2 = (f32[4,64,256]{2,1,0:T(8,128)S(1)}, f32[4,64,256]{2,1,0:T(8,128)}, u32[]{:S(2)}) copy-start(f32[4,64,256]{2,1,0:T(8,128)} %get-tuple-element.15) | copy-start | bytes 786436
  70.6 1.0 %copy-start.1 = (f32[4,64,256]{2,1,0:T(8,128)S(1)}, f32[4,64,256]{2,1,0:T(8,128)}, u32[]{:S(2)}) copy-start(f32[4,64,256]{2,1,0:T(8,128)} %get-tuple-element.16) | copy-start | bytes 786436
  71.6 1.0 %copy-start = (f32[4,64,256]{2,1,0:T(8,128)S(1)}, f32[4,64,256]{2,1,0:T(8,128)}, u32[]{:S(2)}) copy-start(f32[4,64,256]{2,1,0:T(8,128)} %get-tuple-element.17) | copy-start | bytes 786436
  72.7 0.7 copy-start.5
  73.4 0.7 copy-start.4
  74.0 0.7 copy-start.3

commit v2 on v1

--- a/solution.py
+++ b/solution.py
@@ -160,7 +160,7 @@
     )
 
 
-TILE = 512
+TILE = 1024
 SLICE = 64
 TAIL = 16
 
@@ -176,22 +176,17 @@
 def fused_kernel(
     experts,
     live_ref,
+    features_hbm,
+    cotangents_hbm,
+    routes_ref,
+    weights_hbm,
+    biases_ref,
+    input_grads_ref,
+    share_ref,
+    bias_share_ref,
+    master,
     features_ref,
     cotangents_ref,
-    routes_ref,
-    weights_ref,
-    biases_ref,
-    first_ref,
-    second_ref,
-    bias_first_ref,
-    bias_second_ref,
-    input_grads_ref,
-    new_weights_ref,
-    new_first_ref,
-    new_second_ref,
-    new_biases_ref,
-    new_bias_first_ref,
-    new_bias_second_ref,
     low,
     bias_all,
     onehot,
@@ -216,6 +211,7 @@
     core_sems,
     chip_sems,
     line_sems,
+    load_sems,
 ):
     rows, width = features_ref.shape
     wide = experts * width
@@ -230,15 +226,18 @@
     def along(d):
         return {"expert": lax.rem(expert + d, experts)}
 
-    def before(d):
-        return lax.rem(expert + d, experts)
-
     barrier = pltpu.get_barrier_semaphore()
     for peer in [other_core, other_chip] + [along(d) for d in others]:
         pl.semaphore_signal(barrier, inc=1, device_id=peer, device_id_type=pl.DeviceIdType.MESH)
-    for layer in range(LAYERS):
-        low[layer, expert] = weights_ref[layer].astype(jnp.bfloat16)
-    bias_all[expert] = jnp.concatenate([biases_ref[...], jnp.zeros_like(biases_ref)], 0)
+    loads = [
+        pltpu.make_async_copy(weights_hbm.at[layer], master.at[layer], load_sems.at[layer])
+        for layer in range(LAYERS)
+    ]
+    loads.append(pltpu.make_async_copy(features_hbm, features_ref, load_sems.at[LAYERS]))
+    loads.append(pltpu.make_async_copy(cotangents_hbm, cotangents_ref, load_sems.at[LAYERS + 1]))
+    for load in loads:
+        load.start()
+    bias_all[0] = jnp.concatenate([biases_ref[...], jnp.zeros_like(biases_ref)], 0)
     pl.semaphore_wait(barrier, experts + 1)
 
     started = []
@@ -258,48 +257,58 @@
 
     own_start = pl.multiple_of(core * 2 * SLICE + chip * SLICE, SLICE)
     half_start = pl.multiple_of(core * 2 * SLICE, 2 * SLICE)
-    bias_copies = []
+    whole = bias_all.at[0]
+    bias_copies = [
+        send(whole, bias_all.at[experts - d], b_sems, (d - 1,), along(d)) for d in others
+    ]
     line_copies = []
     for layer in range(LAYERS):
-        quarter = low.at[layer, expert, pl.ds(own_start, SLICE)]
-        line_copies.append([send(quarter, quarter, z_sems, (layer, d - 1), along(d)) for d in others])
-        if layer == 0:
-            whole = bias_all.at[expert]
-            bias_copies = [send(whole, whole, b_sems, (d - 1,), along(d)) for d in others]
+        loads[layer].wait()
+        low[layer, 0] = master[layer].astype(jnp.bfloat16)
+        line_copies.append(
+            [
+                send(
+                    low.at[layer, 0, pl.ds(own_start, SLICE)],
+                    low.at[layer, experts - d, pl.ds(own_start, SLICE)],
+                    z_sems,
+                    (layer, d - 1),
+                    along(d),
+                )
+                for d in others
+            ]
+        )
 
     chip_copies = {}
     core_copies = {}
 
     def pass_to_chip(layer):
         chip_copies[layer] = []
-        for copy in line_copies[layer]:
-            copy.wait_recv()
         for d in others:
-            part = low.at[layer, before(d), pl.ds(own_start, SLICE)]
+            line_copies[layer][experts - d - 1].wait_recv()
+            part = low.at[layer, d, pl.ds(own_start, SLICE)]
             chip_copies[layer].append(send(part, part, x_sems, (layer, d - 1), other_chip))
 
     def pass_to_core(layer):
         core_copies[layer] = []
-        for copy in chip_copies[layer]:
-            copy.wait_recv()
         for d in others:
-            part = low.at[layer, before(d), pl.ds(half_start, 2 * SLICE)]
+            chip_copies[layer][d - 1].wait_recv()
+            part = low.at[layer, d, pl.ds(half_start, 2 * SLICE)]
             core_copies[layer].append(send(part, part, c_sems, (layer, d - 1), other_core))
 
     def arrived(layer):
         for copy in core_copies[layer]:
             copy.wait_recv()
 
-    def each_tile(body):
+    def each_tile(body, first=0, last=tiles):
         def step(i, carry):
             body(pl.ds(pl.multiple_of(i * TILE, TILE), TILE))
             return carry
 
-        lax.fori_loop(0, tiles, step, 0)
+        lax.fori_loop(first, last, step, 0)
 
     row_of = lax.broadcasted_iota(jnp.int32, (16, rows), 0)
     position = lax.broadcasted_iota(jnp.int32, (16, rows), 1)
-    named = (routes_ref[...] == row_of % experts) & (row_of < 3 * experts)
+    named = (routes_ref[...] == (row_of + expert) % experts) & (row_of < 3 * experts)
     named = named & (position < live_ref[0])
     onehot[...] = jnp.where(named, 1.0, 0.0).astype(jnp.bfloat16)
     spread_row = lax.broadcasted_iota(jnp.int32, (16, wide), 0)
@@ -329,12 +338,16 @@
                 chosen, bias_parts[layer], contract_rows, preferred_element_type=jnp.float32
             )
 
-    each_tile(prepare)
-
-    def separated(block, at):
-        return jnp.concatenate([block] * experts, 1) * mask[at, :]
-
-    def forward(layer):
+    half = tiles // 2
+    each_tile(prepare, 0, half)
+    pass_to_chip(0)
+    each_tile(prepare, half)
+
+    def separated(block, at, slots=range(experts)):
+        columns = slice(slots[0] * width, (slots[-1] + 1) * width)
+        return jnp.concatenate([block] * len(slots), 1) * mask[at, columns]
+
+    def forward(layer, first=0, last=tiles):
         def body(at):
             block = features_ref[at, :] if layer == 0 else acts[layer - 1, at, :]
             preact = (
@@ -349,42 +362,52 @@
             acts[layer, at, :] = soft.astype(jnp.bfloat16)
             sigs[layer, at, :] = sig
 
-        each_tile(body)
-
-    pass_to_chip(0)
+        each_tile(body, first, last)
+
     pass_to_chip(1)
     pass_to_core(0)
+    loads[LAYERS].wait()
     arrived(0)
-    forward(0)
+    forward(0, 0, half)
     pass_to_chip(2)
     pass_to_core(1)
+    forward(0, half)
     pass_to_chip(3)
     arrived(1)
-    forward(1)
+    forward(1, 0, half)
     pass_to_core(2)
+    forward(1, half)
     pass_to_core(3)
     arrived(2)
     forward(2)
-    arrived(3)
+    loads[LAYERS + 1].wait()
 
     def adjoint_of(layer, at):
         return cotangents_ref[at, :] if layer == LAYERS - 1 else adj[at, :]
 
-    def gradients(layer):
-        grad[...] = jnp.zeros_like(grad)
-        bias_grad[layer] = jnp.zeros((16, width), jnp.float32)
+    groups = (range(experts // 2, experts), range(0, experts // 2))
+
+    def gradients(layer, slots=range(experts)):
+        columns = slice(slots[0] * width, (slots[-1] + 1) * width)
+        grad[:, columns] = jnp.zeros((width, len(slots) * width), jnp.float32)
+        with_bias = slots[-1] == experts - 1
+        if with_bias:
+            bias_grad[layer] = jnp.zeros((16, width), jnp.float32)
 
         def body(at):
             block = adjoint_of(layer, at)
             act = features_ref[at, :] if layer == 0 else acts[layer - 1, at, :]
-            grad[...] += lax.dot_general(
-                act, separated(block, at), contract_rows, preferred_element_type=jnp.float32
+            grad[:, columns] += lax.dot_general(
+                act, separated(block, at, slots), contract_rows, preferred_element_type=jnp.float32
             )
-            bias_grad[layer] += jnp.dot(onehot[:, at], block, preferred_element_type=jnp.float32)
+            if with_bias:
+                bias_grad[layer] += jnp.dot(
+                    onehot[:, at], block, preferred_element_type=jnp.float32
+                )
 
         each_tile(body)
 
-    def pull(layer):
+    def pull(layer, first=0, last=tiles):
         def body(at):
             parts = separated(adjoint_of(layer, at), at)
             pulled = sum(
@@ -401,15 +424,16 @@
             else:
                 input_grads_ref[at, :] = pulled.astype(jnp.bfloat16)
 
-        each_tile(body)
+        each_tile(body, first, last)
 
     def height(layer):
         return SLICE + (TAIL if layer == 0 else 0)
 
     sums = {}
 
-    def share_core(layer):
-        for e in range(experts):
+    def share_core(layer, group):
+        slots = groups[group]
+        for e in slots:
             columns = slice(e * width, (e + 1) * width)
             if layer == 0:
                 tail = jnp.concatenate(
@@ -425,107 +449,162 @@
                 if layer == 0:
                     core_keep[layer, c, e, SLICE:] = tail
                     core_send[layer, c, e, SLICE:] = tail.astype(jnp.bfloat16)
+        held = pl.ds(slots[0], len(slots))
         part = pl.ds(0, height(layer))
-        sums["core", layer] = send(
-            core_send.at[layer, :, :, part],
-            core_recv.at[layer, :, :, part],
+        sums["core", layer, group] = send(
+            core_send.at[layer, :, held, part],
+            core_recv.at[layer, :, held, part],
             core_sems,
-            (layer,),
+            (layer, group),
             other_core,
         )
 
-    def share_chip(layer):
-        sums["core", layer].wait_recv()
+    def share_chip(layer, group):
+        sums["core", layer, group].wait_recv()
         n = height(layer)
-        for e in range(experts):
+        slots = groups[group]
+        for e in slots:
             chip_send[layer, e, :n] = (
                 core_keep[layer, 1 - chip, e, :n]
                 + core_recv[layer, 1 - chip, e, :n].astype(jnp.float32)
             ).astype(jnp.bfloat16)
+        held = pl.ds(slots[0], len(slots))
         part = pl.ds(0, n)
-        sums["chip", layer] = send(
-            chip_send.at[layer, :, part], chip_recv.at[layer, :, part], chip_sems, (layer,), other_chip
-        )
-        for e in range(experts):
+        sums["chip", layer, group] = send(
+            chip_send.at[layer, held, part],
+            chip_recv.at[layer, held, part],
+            chip_sems,
+            (layer, group),
+            other_chip,
+        )
+        for e in slots:
             chip_keep[layer, e, :n] = core_keep[layer, chip, e, :n] + core_recv[
                 layer, chip, e, :n
             ].astype(jnp.float32)
 
-    def share_line(layer):
-        sums["chip", layer].wait_recv()
+    def share_line(layer, group):
+        sums["chip", layer, group].wait_recv()
         n = height(layer)
-        for e in range(experts):
-            total = chip_keep[layer, e, :n] + chip_recv[layer, e, :n].astype(jnp.float32)
-            chip_keep[layer, e, :n] = total
-            line_send[layer, e, :n] = total.astype(jnp.bfloat16)
         part = pl.ds(0, n)
-        sums["line", layer] = [
-            send(
-                line_send.at[layer, before(d), part],
-                line_recv.at[layer, d - 1, part],
-                line_sems,
-                (layer, d - 1),
-                along(d),
-            )
-            for d in others
-        ]
+        for d in groups[group]:
+            total = chip_keep[layer, d, :n] + chip_recv[layer, d, :n].astype(jnp.float32)
+            if d == 0:
+                chip_keep[layer, d, :n] = total
+            else:
+                line_send[layer, d, :n] = total.astype(jnp.bfloat16)
+                sums["line", layer, d] = send(
+                    line_send.at[layer, d, part],
+                    line_recv.at[layer, d - 1, part],
+                    line_sems,
+                    (layer, d - 1),
+                    along(d),
+                )
 
     def finish(layer):
-        for copy in sums["line", layer]:
-            copy.wait_recv()
         n = height(layer)
-        total = chip_keep[layer, expert, :n]
+        total = chip_keep[layer, 0, :n]
         for d in others:
+            sums["line", layer, d].wait_recv()
             total = total + line_recv[layer, d - 1, :n].astype(jnp.float32)
-        master = weights_ref[layer, pl.ds(pl.multiple_of(replica * SLICE, SLICE), SLICE), :]
-        updated, one, two = adam_update(master, first_ref[layer], second_ref[layer], total[:SLICE])
-        new_weights_ref[layer] = updated
-        new_first_ref[layer] = one
-        new_second_ref[layer] = two
+        share_ref[layer] = total[:SLICE]
         if layer == 0:
-
-            def own_columns(block):
-                picked = block[:, :SLICE]
-                for k in range(1, width // SLICE):
-                    picked = jnp.where(replica == k, block[:, k * SLICE : (k + 1) * SLICE], picked)
-                return picked
-
-            updated, one, two = adam_update(
-                own_columns(biases_ref[...]),
-                bias_first_ref[...],
-                bias_second_ref[...],
-                own_columns(total[SLICE : SLICE + LAYERS]),
-            )
-            new_biases_ref[...] = updated
-            new_bias_first_ref[...] = one
-            new_bias_second_ref[...] = two
+            bias_share_ref[...] = total[SLICE : SLICE + 2 * LAYERS]
 
     gradients(3)
-    share_core(3)
+    share_core(3, 0)
+    share_core(3, 1)
+    arrived(3)
     pull(3)
-    share_chip(3)
+    share_chip(3, 0)
+    share_chip(3, 1)
     gradients(2)
-    share_core(2)
-    share_line(3)
+    share_core(2, 0)
+    share_core(2, 1)
+    share_line(3, 0)
+    share_line(3, 1)
     pull(2)
-    share_chip(2)
+    share_chip(2, 0)
+    share_chip(2, 1)
     gradients(1)
-    share_core(1)
-    share_line(2)
+    share_core(1, 0)
+    share_core(1, 1)
+    share_line(2, 0)
+    share_line(2, 1)
     pull(1)
-    share_chip(1)
-    gradients(0)
-    share_core(0)
-    share_line(1)
-    pull(0)
-    share_chip(0)
+    share_chip(1, 0)
+    share_chip(1, 1)
+    gradients(0, groups[0])
+    share_core(0, 0)
+    gradients(0, groups[1])
+    share_core(0, 1)
+    share_chip(0, 0)
+    share_line(1, 0)
+    share_line(1, 1)
+    pull(0, 0, half)
+    share_chip(0, 1)
+    share_line(0, 0)
+    pull(0, half)
     finish(3)
+    share_line(0, 1)
     finish(2)
-    share_line(0)
     finish(1)
     finish(0)
     for copy in started:
         copy.wait_send()
+
+
+def adam_kernel(
+    grads_hbm,
+    weights_hbm,
+    biases_ref,
+    share_ref,
+    bias_share_ref,
+    first_ref,
+    second_ref,
+    bias_first_ref,
+    bias_second_ref,
+    input_grads_hbm,
+    new_weights_ref,
+    new_first_ref,
+    new_second_ref,
+    new_biases_ref,
+    new_bias_first_ref,
+    new_bias_second_ref,
+    master,
+    sems,
+):
+    replica = lax.axis_index("replica")
+    width = biases_ref.shape[1]
+    rows = pl.ds(pl.multiple_of(replica * SLICE, SLICE), SLICE)
+    fetch = pltpu.make_async_copy(weights_hbm.at[:, rows], master, sems.at[0])
+    fetch.start()
+    moved = pltpu.make_async_copy(grads_hbm, input_grads_hbm, sems.at[1])
+    moved.start()
+
+    def own_columns(block):
+        picked = block[:, :SLICE]
+        for k in range(1, width // SLICE):
+            picked = jnp.where(replica == k, block[:, k * SLICE : (k + 1) * SLICE], picked)
+        return picked
+
+    updated, one, two = adam_update(
+        own_columns(biases_ref[...]),
+        bias_first_ref[...],
+        bias_second_ref[...],
+        own_columns(bias_share_ref[:LAYERS]),
+    )
+    new_biases_ref[...] = updated
+    new_bias_first_ref[...] = one
+    new_bias_second_ref[...] = two
+    fetch.wait()
+    for layer in range(LAYERS):
+        updated, one, two = adam_update(
+            master[layer], first_ref[layer], second_ref[layer], share_ref[layer]
+        )
+        new_weights_ref[layer] = updated
+        new_first_ref[layer] = one
+        new_second_ref[layer] = two
+    moved.wait()
 
 
 def fused_shards(
@@ -548,20 +627,27 @@
     vmem = pl.BlockSpec(memory_space=pltpu.VMEM)
     moment = jax.ShapeDtypeStruct(first_moment.shape[1:], f32)
     bias_moment = jax.ShapeDtypeStruct(bias_first.shape[1:], f32)
-    outs = pl.pallas_call(
+    anywhere = pl.BlockSpec(memory_space=pl.ANY)
+    grads, share, bias_share = pl.pallas_call(
         functools.partial(fused_kernel, experts),
         out_shape=(
             jax.ShapeDtypeStruct((rows, width), bf16),
             moment,
-            moment,
-            moment,
-            bias_moment,
-            bias_moment,
-            bias_moment,
+            jax.ShapeDtypeStruct((2 * LAYERS, width), f32),
         ),
-        in_specs=[pl.BlockSpec(memory_space=pltpu.SMEM)] + [vmem] * 9,
-        out_specs=(vmem,) * 7,
+        in_specs=[
+            pl.BlockSpec(memory_space=pltpu.SMEM),
+            anywhere,
+            anywhere,
+            vmem,
+            anywhere,
+            vmem,
+        ],
+        out_specs=(vmem,) * 3,
         scratch_shapes=[
+            pltpu.VMEM((LAYERS, width, width), f32),
+            pltpu.VMEM((rows, width), bf16),
+            pltpu.VMEM((rows, width), bf16),
             pltpu.VMEM((LAYERS, experts, width, width), bf16),
             pltpu.VMEM((experts, 2 * LAYERS, width), f32),
             pltpu.VMEM((16, rows), bf16),
@@ -583,9 +669,10 @@
             pltpu.SemaphoreType.DMA((2, LAYERS, experts - 1)),
             pltpu.SemaphoreType.DMA((2, LAYERS, experts - 1)),
             pltpu.SemaphoreType.DMA((2, experts - 1)),
-            pltpu.SemaphoreType.DMA((2, LAYERS)),
-            pltpu.SemaphoreType.DMA((2, LAYERS)),
+            pltpu.SemaphoreType.DMA((2, LAYERS, 2)),
+            pltpu.SemaphoreType.DMA((2, LAYERS, 2)),
             pltpu.SemaphoreType.DMA((2, LAYERS, experts - 1)),
+            pltpu.SemaphoreType.DMA((LAYERS + 2,)),
         ],
         compiler_params=pltpu.CompilerParams(
             collective_id=0, has_side_effects=True, vmem_limit_bytes=56 * 1024 * 1024
@@ -600,6 +687,30 @@
         routes.reshape(1, rows),
         weights[0],
         biases[0],
+    )
+    outs = pl.pallas_call(
+        adam_kernel,
+        out_shape=(
+            jax.ShapeDtypeStruct((rows, width), bf16),
+            moment,
+            moment,
+            moment,
+            bias_moment,
+            bias_moment,
+            bias_moment,
+        ),
+        in_specs=[anywhere, anywhere] + [vmem] * 7,
+        out_specs=(anywhere,) + (vmem,) * 6,
+        scratch_shapes=[
+            pltpu.VMEM((LAYERS, SLICE, width), f32),
+            pltpu.SemaphoreType.DMA((2,)),
+        ],
+    )(
+        grads,
+        weights[0],
+        biases[0],
+        share,
+        bias_share,
         first_moment[0],
         second_moment[0],
         bias_first[0],

time: 75.6 us -> 95.4 us (1.26)
  Pallas kernels: 67 us -> 93.7 us
  local copies, waits for them, and re-layouts: 7.02 us -> 0 us
    pallas_call x0 -> x1, Pallas kernels: none -> 34.9 us  [fused_shards(): pl.pallas_call(adam_kernel, out_shape=(jax.ShapeDtypeStruct((rows, width)...]
    pallas_call x1, Pallas kernels: 67 us -> 58.8 us  [fused_shards(): pl.pallas_call(functools.partial(fused_kernel, experts), out_shape=(jax.S...]
    unnamed x19 -> x0, local copies, waits for them, and re-layouts: 7.02 us -> none
where the time goes in v2:
time: 95.4 us; the launch traced here: 95.1 us
  Pallas kernels  93.7 us (98%)
  between operations  1.45 us (2%)
    pallas_call x1, Pallas kernels, fused_shards(): pl.pallas_call(functools.partial(fused_kernel, experts), out_shape=(jax.S...  58.8 us
    pallas_call x1, Pallas kernels, fused_shards(): pl.pallas_call(adam_kernel, out_shape=(jax.ShapeDtypeStruct((rows, width)...  34.9 us

profile of v2, /device:TPU:0, one launch (start us, length us, event | category | flops | bytes accessed | tf_op | source)
XLA Modules:
  0.0 95.1 jit_solution(59703362017612339)
XLA Ops:
  1.3 58.8 %shard_map.153 = (bf16[2048,256]{1,0:T(8,128)(2,1)}, f32[4,64,256]{2,1,0:T(8,128)}, f32[8,256]{1,0:T(8,128)}) custom-call(s32[1]{0:T(128)S(6)} %copy.17.live_ref, bf16[2048,256]{1,0:T(8,128)(2,1)} %features_hbm.1, bf16[2048,256]{1,0:T(8,128)(2,1)} %cotangents_hbm.1, s32[1,2048]{1,0:T(1,128)} %bitcast.24, f32[4,256,256]{2,1,0:T(8,128)} %bitcast.13, ...), custom_call_target="tpu_custom_call" | custom-call | flops 11811160064 | bytes 6291456 | tf_op jit(solution)/shard_map/pallas_call | solution.py:631
  60.0 34.9 %shard_map.154 = (bf16[2048,256]{1,0:T(8,128)(2,1)}, f32[4,64,256]{2,1,0:T(8,128)}, f32[4,64,256]{2,1,0:T(8,128)}, f32[4,64,256]{2,1,0:T(8,128)}, f32[4,64]{1,0:...) custom-call(bf16[2048,256]{1,0:T(8,128)(2,1)} %get-tuple-element.17.grads_hbm, f32[4,256,256]{2,1,0:T(8,128)} %bitcast.14, ...), custom_call_target="tpu_custom_call" | custom-call | tf_op jit(solution)/shard_map/pallas_call | solution.py:691

commit v3 on v2

--- a/solution.py
+++ b/solution.py
@@ -162,6 +162,7 @@
 
 TILE = 1024
 SLICE = 64
+CHUNKS = LAYERS
 TAIL = 16
 
 
@@ -571,6 +572,7 @@
     new_bias_first_ref,
     new_bias_second_ref,
     master,
+    passing,
     sems,
 ):
     replica = lax.axis_index("replica")
@@ -578,8 +580,18 @@
     rows = pl.ds(pl.multiple_of(replica * SLICE, SLICE), SLICE)
     fetch = pltpu.make_async_copy(weights_hbm.at[:, rows], master, sems.at[0])
     fetch.start()
-    moved = pltpu.make_async_copy(grads_hbm, input_grads_hbm, sems.at[1])
-    moved.start()
+    chunk = grads_hbm.shape[0] // CHUNKS
+    parts = [pl.ds(k * chunk, chunk) for k in range(CHUNKS)]
+    inward = [
+        pltpu.make_async_copy(grads_hbm.at[part], passing.at[part], sems.at[1 + k])
+        for k, part in enumerate(parts)
+    ]
+    outward = [
+        pltpu.make_async_copy(passing.at[part], input_grads_hbm.at[part], sems.at[1 + CHUNKS + k])
+        for k, part in enumerate(parts)
+    ]
+    for copy in inward:
+        copy.start()
 
     def own_columns(block):
         picked = block[:, :SLICE]
@@ -604,7 +616,10 @@
         new_weights_ref[layer] = updated
         new_first_ref[layer] = one
         new_second_ref[layer] = two
-    moved.wait()
+        inward[layer].wait()
+        outward[layer].start()
+    for copy in outward:
+        copy.wait()
 
 
 def fused_shards(
@@ -703,7 +718,8 @@
         out_specs=(anywhere,) + (vmem,) * 6,
         scratch_shapes=[
             pltpu.VMEM((LAYERS, SLICE, width), f32),
-            pltpu.SemaphoreType.DMA((2,)),
+            pltpu.VMEM((rows, width), bf16),
+            pltpu.SemaphoreType.DMA((1 + 2 * CHUNKS,)),
         ],
     )(
         grads,

time: 95.4 us -> 64.6 us (0.68)
  Pallas kernels: 93.7 us -> 63 us
    pallas_call x1, Pallas kernels: 34.9 us -> 4.2 us  [fused_shards(): pl.pallas_call(adam_kernel, out_shape=(jax.ShapeDtypeStruct((rows, width)...]
where the time goes in v3:
time: 64.6 us; the launch traced here: 64.4 us
  Pallas kernels  63 us (98%)
  between operations  1.45 us (2%)
    pallas_call x1, Pallas kernels, fused_shards(): pl.pallas_call(functools.partial(fused_kernel, experts), out_shape=(jax.S...  58.8 us
    pallas_call x1, Pallas kernels, fused_shards(): pl.pallas_call(adam_kernel, out_shape=(jax.ShapeDtypeStruct((rows, width)...  4.2 us

profile of v3, /device:TPU:0, one launch (start us, length us, event | category | flops | bytes accessed | tf_op | source)
XLA Modules:
  0.0 64.4 jit_solution(8491731714237193292)
XLA Ops:
  1.3 58.8 %shard_map.153 = (bf16[2048,256]{1,0:T(8,128)(2,1)}, f32[4,64,256]{2,1,0:T(8,128)}, f32[8,256]{1,0:T(8,128)}) custom-call(s32[1]{0:T(128)S(6)} %copy.17.live_ref, bf16[2048,256]{1,0:T(8,128)(2,1)} %features_hbm.1, bf16[2048,256]{1,0:T(8,128)(2,1)} %cotangents_hbm.1, s32[1,2048]{1,0:T(1,128)} %bitcast.24, f32[4,256,256]{2,1,0:T(8,128)} %bitcast.13, ...), custom_call_target="tpu_custom_call" | custom-call | flops 11811160064 | bytes 6291456 | tf_op jit(solution)/shard_map/pallas_call | solution.py:646
  60.0 4.2 %shard_map.154 = (bf16[2048,256]{1,0:T(8,128)(2,1)}, f32[4,64,256]{2,1,0:T(8,128)}, f32[4,64,256]{2,1,0:T(8,128)}, f32[4,64,256]{2,1,0:T(8,128)}, f32[4,64]{1,0:...) custom-call(bf16[2048,256]{1,0:T(8,128)(2,1)} %get-tuple-element.17.grads_hbm, f32[4,256,256]{2,1,0:T(8,128)} %bitcast.14, ...), custom_call_target="tpu_custom_call" | custom-call | tf_op jit(solution)/shard_map/pallas_call | solution.py:706
